TPU v7x, 512 devices: a whole 4x4x16 slice. The times are simulated.
512 devices in a mesh: seq: 64 (over z, y), head: 8 (over x, core).
Axes of the slice: x: 4, y: 4, z: 16, core: 2. Of those that a mesh axis runs over, the one named last changes fastest.
Arguments:
- inner_acts: bfloat16 [16384, 8192], P('seq', 'head'), may hold values from -0.4375 to 0.4375
- out_grad: bfloat16 [16384, 8192], P('seq', 'head'), may hold values from -0.4375 to 0.4375
- write_proj: bfloat16 [16384, 128], P('seq'), may hold values from -3 to 3
- read_proj: bfloat16 [16384, 128], P('seq'), may hold values from -3 to 3
- log_decay: float32 [16384, 64], P('seq', 'head'), may hold values from -2.5 to 0, as said below
- w_in: bfloat16 [4096, 8192], P('seq', 'head'), may hold values from -0.1875 to 0.1875
Outputs:
- input_grad: bfloat16 [16384, 4096], P('seq', 'head')
- act_grad: bfloat16 [16384, 8192], P('seq', 'head')
- write_grad: float32 [16384, 128], P('seq')
- read_grad: float32 [16384, 128], P('seq')
Inputs may be any that keep to these rules, and one draw needn't show every extreme that they name: `log_decay`: natural log of a decay factor of each head at each token; every entry is negative.
All inputs are finite; a program needn't handle non-finite values.
Results may differ from a plain program's by a relative error of at most 0.019.
Values may be sent and summed in bfloat16 or wider, within the bound.
A program may use at most 192 MiB of HBM per device.

v0:
```python
import jax
import jax.numpy as jnp
from jax import lax
from jax.sharding import PartitionSpec as P

SPAN = 256
exact_mode = lax.Precision.HIGHEST


def carried_in(shard, axis, combine, identity):
    devices, position = (lax.axis_size(axis), lax.axis_index(axis))
    everything = jax.tree.map(
        lambda part, kind: lax.all_gather(part.astype(kind), axis),
        shard,
        (jnp.bfloat16, jnp.bfloat16),
    )
    start = jax.tree.map(
        lambda part, zero: jnp.broadcast_to(jnp.asarray(zero, part.dtype), part.shape),
        shard,
        identity,
    )

    def step(k, before):
        reached = k < position
        new = combine(
            before, jax.tree.map(lambda part, own: part[k].astype(own.dtype), everything, shard)
        )
        return jax.tree.map(lambda a, b: jnp.where(reached, a, b), new, before)

    return lax.fori_loop(0, devices, step, start)


def carried_in_2(part, axis, combine, identity):
    count = lax.axis_size(axis)
    place = lax.axis_index(axis)
    ahead = count - 1 - place
    gathered = jax.tree.map(lambda a: lax.all_gather(a, axis), part)
    state = jax.tree.map(lambda a, e: jnp.zeros_like(a) + jnp.asarray(e, a.dtype), part, identity)

    def one(step, state):
        source = count - 1 - step
        return combine(
            state, jax.tree.map(lambda a: lax.dynamic_index_in_dim(a, source, 0, False), gathered)
        )

    return lax.fori_loop(0, ahead, one, state)


def decay_blocks(cumulative):
    count = cumulative.shape[1]
    by_head = jnp.swapaxes(cumulative, 1, 2)
    spread_log = by_head[:, :, :, None] - by_head[:, :, None, :]
    below_diag = jnp.arange(count)[:, None] >= jnp.arange(count)[None, :]
    return jnp.exp(jnp.where(below_diag, spread_log, -jnp.inf))


def combine(earlier, later):
    return (earlier[0] + later[0], jnp.exp(later[0])[:, None, None] * earlier[1] + later[1])


def local(inner_acts, out_grad, write_proj, read_proj, log_decay, w_in):
    tok_rows = inner_acts.shape[0]
    head_count = log_decay.shape[1]
    head_dim = inner_acts.shape[1] // head_count
    state_dim = write_proj.shape[1]
    blocks = tok_rows // SPAN
    act_narrow = inner_acts.reshape(blocks, SPAN, head_count, head_dim)
    grad_narrow = out_grad.reshape(blocks, SPAN, head_count, head_dim)
    act_blocks = act_narrow.astype(jnp.float32)
    grad_blocks = grad_narrow.astype(jnp.float32)
    write_blocks = write_proj.astype(jnp.float32).reshape(blocks, SPAN, state_dim)
    read_blocks = read_proj.astype(jnp.float32).reshape(blocks, SPAN, state_dim)
    cumulative = jnp.cumsum(log_decay.reshape(blocks, SPAN, head_count), axis=1)
    totals = cumulative[:, -1, :]
    tail_decay = jnp.exp(totals[:, None, :] - cumulative)
    head_decay = jnp.exp(cumulative)
    decays = decay_blocks(cumulative)
    weighted = decays * jnp.einsum(
        "kahp,kbhp->khab", grad_narrow, act_narrow, preferred_element_type=jnp.float32
    )
    read_local = jnp.einsum("khab,kbn->kan", weighted, write_blocks, precision=exact_mode)
    write_local = jnp.einsum("khab,kan->kbn", weighted, read_blocks, precision=exact_mode)
    scores = jnp.einsum(
        "kan,kbn->kab",
        read_proj.reshape(blocks, SPAN, state_dim),
        write_proj.reshape(blocks, SPAN, state_dim),
        preferred_element_type=jnp.float32,
    )
    act_local = jnp.einsum(
        "khab,kahp->kbhp", decays * scores[:, None], grad_blocks, precision=exact_mode
    )
    block_ends = jnp.einsum(
        "kbhp,kbn->khpn", act_blocks * tail_decay[..., None], write_blocks, precision=exact_mode
    )
    fronts = jnp.einsum(
        "kahp,kan->khpn", grad_blocks * head_decay[..., None], read_blocks, precision=exact_mode
    )
    zero_log = jnp.zeros((head_count,), jnp.float32)
    zero_state = jnp.zeros((head_count, head_dim, state_dim), jnp.float32)
    prefix_logs = []
    prefix_states = []
    running = (zero_log, zero_state)
    index = 0
    prefix_logs.append(running[0])
    prefix_states.append(running[1])
    running = combine(running, (totals[index], block_ends[index]))
    end_log, end_state = running
    suffix_logs = [zero_log] * blocks
    suffix_grads = [zero_state] * blocks
    running = (zero_log, zero_state)
    for index in reversed(range(blocks)):
        suffix_logs[index] = running[0]
        suffix_grads[index] = running[1]
        running = combine(running, (totals[index], fronts[index]))
    front_log, front_state = running
    state_in = carried_in((end_log, end_state), "seq", combine, (zero_log, zero_state))[1]
    grad_in = carried_in_2((front_log, front_state), "seq", combine, (zero_log, zero_state))[1]
    current = state_in
    index = 0
    states_list = [current]
    grads_list = [zero_state] * blocks
    current = grad_in
    for index in reversed(range(blocks)):
        grads_list[index] = current
        current = jnp.exp(totals[index])[:, None, None] * current + fronts[index]
    state_stack = jnp.stack(states_list)
    grad_stack = jnp.stack(grads_list)
    read_carry = jnp.einsum(
        "kahp,khpn->kan", grad_blocks * head_decay[..., None], state_stack, precision=exact_mode
    )
    write_carry = jnp.einsum(
        "kbhp,khpn->kbn", act_blocks * tail_decay[..., None], grad_stack, precision=exact_mode
    )
    act_carry = (
        jnp.einsum("khpn,kbn->kbhp", grad_stack, write_blocks, precision=exact_mode)
        * tail_decay[..., None]
    )
    act_grad = (act_local + act_carry).astype(jnp.bfloat16).reshape(tok_rows, head_count * head_dim)
    write_part = (write_local + write_carry).reshape(tok_rows, state_dim)
    read_part = (read_local + read_carry).reshape(tok_rows, state_dim)
    write_grad, read_grad = (
        lax.psum(write_part.astype(jnp.bfloat16), "head").astype(jnp.float32),
        lax.psum(read_part.astype(jnp.bfloat16), "head").astype(jnp.float32),
    )
    group_term = lax.dot_general(
        act_grad,
        lax.all_gather(w_in, "seq", axis=0, tiled=True),
        (((1,), (1,)), ((), ())),
        preferred_element_type=jnp.float32,
    )
    input_grad = lax.psum_scatter(
        group_term.astype(jnp.bfloat16).astype(jnp.float32).astype(jnp.bfloat16),
        "head",
        scatter_dimension=1,
        tiled=True,
    )
    return (input_grad, act_grad, write_grad, read_grad)


def solution(mesh):
    return jax.shard_map(
        local,
        mesh=mesh,
        in_specs=(
            P("seq", "head"),
            P("seq", "head"),
            P("seq", None),
            P("seq", None),
            P("seq", "head"),
            P("seq", "head"),
        ),
        out_specs=(P("seq", "head"), P("seq", "head"), P("seq", None), P("seq", None)),
        check_vma=False,
    )
```

profile of v0, /device:TPU:8, one launch (start us, length us, event | category | flops | bytes accessed | tf_op | source)
XLA Modules:
  0.0 784.8 jit_solution(3327351343411042735)
XLA Ops:
  7.2 1.3 reduce-window.6
  11.4 1.3 fusion.14
  13.1 1.8 convolution_add_fusion.1
  17.9 85.3 %all-gather = f32[64,1,8]{2,1,0:T(1,128)} all-gather(f32[1,1,8]{2,1,0:T(1,128)S(1)} %copy-done.7), channel_id=2, replica_groups=mesh['seq'=64,'head'=8] {'seq'}, dimensions={0}, use_global_device_ids=true | all-gather | bytes 2080 | tf_op jit(solution)/shard_map/all_gather | solution.py:37
  104.5 73.1 %all-gather.3 = bf16[64,1,8]{2,1,0:T(2,128)(2,1)S(1)} all-gather(bf16[1,1,8]{2,1,0:T(2,128)(2,1)} %slice.19), channel_id=5, replica_groups=mesh['seq'=64,'head'=8] {'seq'}, dimensions={0}, use_global_device_ids=true | all-gather | bytes 1040 | tf_op jit(solution)/shard_map/all_gather | solution.py:13
  178.2 1.7 multiply_reduce_fusion
  179.9 30.1 %all-gather.12.cloned.1.call-done = bf16[512,128,128]{2,1,0:T(8,128)(2,1)} async-done(((bf16[8,128,128]{2,1,0:T(8,128)(2,1)}), bf16[512,128,128]{2,1,0:T(8,128)(2,1)}) %all-gather.12.cloned.1.call-update) | async-done | bytes 16777232 | tf_op jit(solution)/shard_map/all_gather | solution.py:13
  210.0 115.6 %while.29 = (s32[]{:T(128)}, f32[8,128,128]{2,1,0:T(8,128)S(1)}, s32[]{:T(128)}, bf16[64,8]{1,0:T(8,128)(2,1)}, bf16[64,8,128,128]{3,2,1,0:T(8,128)(2,1)}, /*index=5*/s32[]{:T(128)}, s32[]{:T(128)}) while((s32[]{:T(128)}, f32[8,128,128]{2,1,0:T(8,128)S(1)}, s32[]{:T(128)}, bf16[64,8]{1,0:T(8,128)(2,1)}, ...), condition=%wide.region_8.9_spmd.clone, body=%wide.region_7.8_spmd.clone.sunk | while | flops 655372 | bytes 1310905 | solution.py:30
  327.6 176.6 %all-gather.10.cloned.1.call-done = f32[512,128,128]{2,1,0:T(8,128)} async-done(((f32[8,128,128]{2,1,0:T(8,128)}), f32[512,128,128]{2,1,0:T(8,128)}) %all-gather.10.cloned.1.call-update) | async-done | bytes 33554448 | tf_op jit(solution)/shard_map/all_gather | solution.py:37
  504.3 118.4 %while.28 = (s32[]{:T(128)}, f32[8,128,128]{2,1,0:T(8,128)S(1)}, s32[]{:T(128)}, f32[64,8]{1,0:T(8,128)}, f32[64,8,128,128]{3,2,1,0:T(8,128)}, /*index=5*/s32[]{:T(128)}, s32[]{:T(128)}, s32[]{:T(128)}, s32[]{:T(128)}) while((s32[]{:T(128)}, f32[8,128,128]{2,1,0:T(8,128)S(1)}, s32[]{:T(128)}, f32[64,8]{1,0:T(8,128)}, ...), condition=%wide.region_3.4_spmd, body=%wide.region_2.3_spmd.sunk | while | flops 262150 | bytes 1573107 | solution.py:46
  590.7 1.3 bitcast_add_fusion.5
  600.4 1.2 bitcast_add_fusion.5
  606.1 1.2 bitcast_add_fusion.5
  615.7 1.2 bitcast_add_fusion.5
  619.5 1.2 bitcast_add_fusion.5
  621.4 1.2 bitcast_add_fusion.5
  623.3 1.8 convolution_bitcast_fusion.2
  626.1 2.4 fusion.11
  628.8 31.9 %all-gather.8.cloned.1.call-done = bf16[4096,1024]{1,0:T(8,128)(2,1)} async-done(((bf16[64,1024]{1,0:T(8,128)(2,1)}), bf16[4096,1024]{1,0:T(8,128)(2,1)}) %all-gather.8.cloned.1.call-update) | async-done | bytes 8388624 | tf_op jit(solution)/shard_map/all_gather | solution.py:147
  660.7 7.1 convolution_convert_fusion
  668.8 65.5 %all-reduce.3.cloned.1.call-done = (bf16[256,128]{1,0:T(8,128)(2,1)}, bf16[256,128]{1,0:T(8,128)(2,1)}) async-done(((bf16[256,128]{1,0:T(8,128)(2,1)}, bf16[256,128]{1,0:T(8,128)(2,1)}), (bf16[256,128]{1,0:T(8,128)(2,1)}, bf16[256,128]{1,0:T(8,128)(2,1)})) %all-reduce.3.cloned.1.call-update) | async-done | bytes 131088 | tf_op jit(solution)/shard_map/psum | solution.py:142
  734.3 1.5 convert_element_type.84
  735.8 1.5 convert_element_type.89
  737.3 40.9 %reduce-scatter.2.cloned.1.call-done = bf16[256,512]{1,0:T(8,128)(2,1)} async-done(((bf16[256,4096]{1,0:T(8,128)(2,1)}), bf16[256,512]{1,0:T(8,128)(2,1)}) %reduce-scatter.2.cloned.1.call-update) | async-done | bytes 262160 | tf_op jit(solution)/shard_map/reduce_scatter | solution.py:151
  (300 shorter events, 236.6 us)
Async XLA Ops:
  7.2 3.9 copy-start
  7.2 3.3 copy-start.3
  7.2 202.8 %all-gather.12.cloned.1.call-start = ((), (), s32[]{:S(2)}) async-start(), calls=%async_computation.4 | async-start | bytes 17039360 | tf_op jit(solution)/shard_map/all_gather | solution.py:13
  8.8 1.8 copy-start.4
  10.7 0.7 copy-start.6
  10.7 2.4 copy-start.1
  10.7 2.4 copy-start.2
  12.7 491.5 %all-gather.10.cloned.1.call-start = ((), (), s32[]{:S(2)}) async-start(), calls=%async_computation.3 | async-start | bytes 34078720 | tf_op jit(solution)/shard_map/all_gather | solution.py:37
  13.1 4.8 copy-start.7
  15.0 645.7 %all-gather.8.cloned.1.call-start = ((), (), s32[]{:S(2)}) async-start(), calls=%async_computation.1 | async-start | bytes 8519680 | tf_op jit(solution)/shard_map/all_gather | solution.py:147
  15.7 718.6 %all-reduce.3.cloned.1.call-start = ((), (), s32[]{:S(2)}) async-start(), calls=%async_computation.5 | async-start | bytes 262144 | tf_op jit(solution)/shard_map/psum | solution.py:142
  622.7 3.4 copy-start.5
  628.6 149.7 %reduce-scatter.2.cloned.1.call-start = ((), (), s32[]{:S(2)}) async-start(), calls=%async_computation.2 | async-start | bytes 2359296 | tf_op jit(solution)/shard_map/reduce_scatter | solution.py:151
Sparse Core Ops, SparseCore 0:
  12.8 197.1 all-gather.11
  213.5 290.6 all-gather.9
  507.2 153.4 all-gather.7
  663.5 70.7 all-reduce.2
  737.8 40.4 reduce-scatter.1
where the time goes:
time: 794 us; the launch traced here: 785 us
  waiting for transfers between devices  346 us (44%)
  other arithmetic  195 us (25%)
  blocking collectives  158 us (20%)
  local copies, waits for them, and re-layouts  48 us (6%)
  matrix products  20.7 us (3%)
  between operations  14 us (2%)
    all_gather x1, waiting for transfers between devices, carried_in_2(): gathered = jax.tree.map(lambda a: lax.all_gather(a, axis), part)  177 us
    all_gather x1, blocking collectives, carried_in_2(): gathered = jax.tree.map(lambda a: lax.all_gather(a, axis), part)  85.3 us
    add x62, other arithmetic, combine(): jnp.exp(later[0])[:, None, None] * earlier[1] + later[1]  73.9 us
    all_gather x1, blocking collectives, carried_in(): lax.all_gather(part.astype(kind), axis)  73.1 us
    select_n x64, other arithmetic, step(): return jax.tree.map(lambda a, b: jnp.where(reached, a, b), new, before)  70.1 us
    psum x1, waiting for transfers between devices, local(): lax.psum(write_part.astype(jnp.bfloat16), 'head').astype(jnp.float32)  65.5 us
    exp x64, other arithmetic, combine(): jnp.exp(later[0])[:, None, None] * earlier[1] + later[1]  44.4 us
    exp x62, local copies, waits for them, and re-layouts, combine(): jnp.exp(later[0])[:, None, None] * earlier[1] + later[1]  42.7 us
  transfers between devices with their start and end apart: 5, of which 5 were waited for; matrix products, arithmetic and copies ran while one was open for 33% of the time, Pallas kernels for 0%

commit v1 on v0

--- a/solution.py
+++ b/solution.py
@@ -1,3 +1,4 @@
+import functools
 import jax
 import jax.numpy as jnp
 from jax import lax
@@ -5,6 +6,19 @@
 
 SPAN = 256
 exact_mode = lax.Precision.HIGHEST
+
+
+def test_cycles(mat, net_axis):
+    y = jnp.concatenate(
+        jax.lax.all_to_all(
+            jnp.stack(jax.lax.axis_size(net_axis) * [mat]), net_axis, split_axis=0, concat_axis=0
+        ),
+        axis=0,
+    )
+    return y
+
+
+fix_shapes_in = functools.partial(test_cycles, net_axis="seq")
 
 
 def carried_in(shard, axis, combine, identity):
@@ -143,10 +157,7 @@
         lax.psum(read_part.astype(jnp.bfloat16), "head").astype(jnp.float32),
     )
     group_term = lax.dot_general(
-        act_grad,
-        lax.all_gather(w_in, "seq", axis=0, tiled=True),
-        (((1,), (1,)), ((), ())),
-        preferred_element_type=jnp.float32,
+        act_grad, fix_shapes_in(w_in), (((1,), (1,)), ((), ())), preferred_element_type=jnp.float32
     )
     input_grad = lax.psum_scatter(
         group_term.astype(jnp.bfloat16).astype(jnp.float32).astype(jnp.bfloat16),

time: 794 us -> 1050 us (1.32)
  blocking collectives: 158 us -> 583 us
  waiting for transfers between devices: 346 us -> 154 us
  starting transfers between devices: 0.38 us -> 19.3 us
    all_gather x1, blocking collectives: 73.1 us -> 506 us  [carried_in(): lax.all_gather(part.astype(kind), axis)]
    all_gather x1, waiting for transfers between devices: 177 us -> 56.8 us  [carried_in_2(): gathered = jax.tree.map(lambda a: lax.all_gather(a, axis), part)]
    all_gather x1 -> x0, waiting for transfers between devices: 31.9 us -> none  [local(): lax.all_gather(w_in, 'seq', axis=0, tiled=True)]
    all_gather x1, waiting for transfers between devices: 30.1 us -> 0.02 us  [carried_in(): lax.all_gather(part.astype(kind), axis)]
    all_to_all x0 -> x1, starting transfers between devices: none -> 18.9 us  [test_cycles(): jax.lax.all_to_all(jnp.stack(jax.lax.axis_size(net_axis) * [mat]), net_ax...]
  transfers between devices with their start and end apart: 5 -> 5, of which waited for: 5 -> 3; matrix products, arithmetic and copies ran while one was open for 33% -> 25% of each run, Pallas kernels for 0% -> 0%
where the time goes in v1:
time: 1050 us; the launch traced here: 1040 us
  blocking collectives  583 us (56%)
  other arithmetic  193 us (18%)
  waiting for transfers between devices  154 us (15%)
  local copies, waits for them, and re-layouts  52.1 us (5%)
  matrix products  19.8 us (2%)
  starting transfers between devices  19.3 us (2%)
  between operations  14.1 us (1%)
    all_gather x1, blocking collectives, carried_in(): lax.all_gather(part.astype(kind), axis)  506 us
    all_gather x1, blocking collectives, carried_in_2(): gathered = jax.tree.map(lambda a: lax.all_gather(a, axis), part)  76.8 us
    add x62, other arithmetic, combine(): jnp.exp(later[0])[:, None, None] * earlier[1] + later[1]  73.6 us
    select_n x64, other arithmetic, step(): return jax.tree.map(lambda a, b: jnp.where(reached, a, b), new, before)  70.2 us
    all_gather x1, waiting for transfers between devices, carried_in_2(): gathered = jax.tree.map(lambda a: lax.all_gather(a, axis), part)  56.8 us
    psum x1, waiting for transfers between devices, local(): lax.psum(write_part.astype(jnp.bfloat16), 'head').astype(jnp.float32)  56.1 us
    exp x64, other arithmetic, combine(): jnp.exp(later[0])[:, None, None] * earlier[1] + later[1]  44.4 us
    exp x62, local copies, waits for them, and re-layouts, combine(): jnp.exp(later[0])[:, None, None] * earlier[1] + later[1]  42.6 us
  transfers between devices with their start and end apart: 5, of which 3 were waited for; matrix products, arithmetic and copies ran while one was open for 25% of the time, Pallas kernels for 0%

profile of v1, /device:TPU:8, one launch (start us, length us, event | category | flops | bytes accessed | tf_op | source)
XLA Modules:
  0.0 1038.5 jit_solution(15842452310401971215)
XLA Ops:
  7.2 1.3 reduce-window.6
  11.3 1.3 fusion.14
  13.0 1.8 convolution_add_fusion.1
  14.9 4.3 stack.2
  19.2 18.9 %all-to-all-start = ((bf16[64,64,1024]{2,1,0:T(8,128)(2,1)}), bf16[64,64,1024]{2,1,0:T(8,128)(2,1)}, u32[]{:S(2)}, u32[]{:S(2)}) async-start(bf16[64,64,1024]{2,1,0:T(8,128)(2,1)} %stack.2), calls=%async_computation | async-start | bytes 16777216 | tf_op jit(solution)/shard_map/all_to_all | solution.py:13
  39.4 506.3 %all-gather.3 = bf16[64,1,8]{2,1,0:T(2,128)(2,1)S(1)} all-gather(bf16[1,1,8]{2,1,0:T(2,128)(2,1)} %slice.19), channel_id=5, replica_groups=mesh['seq'=64,'head'=8] {'seq'}, dimensions={0}, use_global_device_ids=true | all-gather | bytes 1040 | tf_op jit(solution)/shard_map/all_gather | solution.py:27
  546.3 76.8 %all-gather = f32[64,1,8]{2,1,0:T(1,128)} all-gather(f32[1,1,8]{2,1,0:T(1,128)} %get-tuple-element.277), channel_id=2, replica_groups=mesh['seq'=64,'head'=8] {'seq'}, dimensions={0}, use_global_device_ids=true | all-gather | bytes 2080 | tf_op jit(solution)/shard_map/all_gather | solution.py:51
  624.1 1.7 multiply_reduce_fusion
  625.8 115.7 %while.29 = (s32[]{:T(128)}, f32[8,128,128]{2,1,0:T(8,128)S(1)}, s32[]{:T(128)}, bf16[64,8]{1,0:T(8,128)(2,1)}, bf16[64,8,128,128]{3,2,1,0:T(8,128)(2,1)}, /*index=5*/s32[]{:T(128)}, s32[]{:T(128)}) while((s32[]{:T(128)}, f32[8,128,128]{2,1,0:T(8,128)S(1)}, s32[]{:T(128)}, bf16[64,8]{1,0:T(8,128)(2,1)}, ...), condition=%wide.region_8.9_spmd.clone, body=%wide.region_7.8_spmd.clone.sunk | while | flops 655372 | bytes 1310905 | solution.py:44
  743.5 56.8 %all-gather.7.cloned.1.call-done = f32[512,128,128]{2,1,0:T(8,128)} async-done(((f32[8,128,128]{2,1,0:T(8,128)}), f32[512,128,128]{2,1,0:T(8,128)}) %all-gather.7.cloned.1.call-update) | async-done | bytes 33554448 | tf_op jit(solution)/shard_map/all_gather | solution.py:51
  800.4 118.0 %while.28 = (s32[]{:T(128)}, f32[8,128,128]{2,1,0:T(8,128)S(1)}, s32[]{:T(128)}, f32[64,8]{1,0:T(8,128)}, f32[64,8,128,128]{3,2,1,0:T(8,128)}, /*index=5*/s32[]{:T(128)}, s32[]{:T(128)}, s32[]{:T(128)}, s32[]{:T(128)}) while((s32[]{:T(128)}, f32[8,128,128]{2,1,0:T(8,128)S(1)}, s32[]{:T(128)}, f32[64,8]{1,0:T(8,128)}, ...), condition=%wide.region_3.4_spmd, body=%wide.region_2.3_spmd.sunk | while | flops 262150 | bytes 1573107 | solution.py:60
  801.1 1.2 bitcast_add_fusion.5
  803.1 1.2 bitcast_add_fusion.5
  818.3 1.2 bitcast_add_fusion.5
  822.1 1.2 bitcast_add_fusion.5
  827.8 1.2 bitcast_add_fusion.5
  833.5 1.2 bitcast_add_fusion.5
  918.5 1.8 convolution_bitcast_fusion.2
  922.2 1.5 fusion.11
  923.7 7.1 convolution_convert_fusion
  931.9 56.1 %all-reduce.3.cloned.1.call-done = (bf16[256,128]{1,0:T(8,128)(2,1)}, bf16[256,128]{1,0:T(8,128)(2,1)}) async-done(((bf16[256,128]{1,0:T(8,128)(2,1)}, bf16[256,128]{1,0:T(8,128)(2,1)}), (bf16[256,128]{1,0:T(8,128)(2,1)}, bf16[256,128]{1,0:T(8,128)(2,1)})) %all-reduce.3.cloned.1.call-update) | async-done | bytes 131088 | tf_op jit(solution)/shard_map/psum | solution.py:156
  988.0 1.5 convert_element_type.84
  989.5 1.5 convert_element_type.89
  991.0 40.9 %reduce-scatter.2.cloned.1.call-done = bf16[256,512]{1,0:T(8,128)(2,1)} async-done(((bf16[256,4096]{1,0:T(8,128)(2,1)}), bf16[256,512]{1,0:T(8,128)(2,1)}) %reduce-scatter.2.cloned.1.call-update) | async-done | bytes 262160 | tf_op jit(solution)/shard_map/reduce_scatter | solution.py:162
  (308 shorter events, 234.5 us)
Async XLA Ops:
  7.2 3.9 copy-start
  7.2 3.3 copy-start.3
  7.2 618.6 %all-gather.9.cloned.1.call-start = ((), (), s32[]{:S(2)}) async-start(), calls=%async_computation.4 | async-start | bytes 17039360 | tf_op jit(solution)/shard_map/all_gather | solution.py:27
  8.8 1.7 copy-start.8
  10.6 0.7 copy-start.11
  10.7 2.4 copy-start.1
  10.7 2.4 copy-start.2
  12.6 2.3 copy-start.5
  12.6 787.7 %all-gather.7.cloned.1.call-start = ((), (), s32[]{:S(2)}) async-start(), calls=%async_computation.3 | async-start | bytes 34078720 | tf_op jit(solution)/shard_map/all_gather | solution.py:51
  19.2 904.5 %all-to-all-start = ((bf16[64,64,1024]{2,1,0:T(8,128)(2,1)}), bf16[64,64,1024]{2,1,0:T(8,128)(2,1)}, u32[]{:S(2)}, u32[]{:S(2)}) async-start(bf16[64,64,1024]{2,1,0:T(8,128)(2,1)} %stack.2), calls=%async_computation | async-start | bytes 16777216 | tf_op jit(solution)/shard_map/all_to_all | solution.py:13
  38.1 949.9 %all-reduce.3.cloned.1.call-start = ((), (), s32[]{:S(2)}) async-start(), calls=%async_computation.5 | async-start | bytes 262144 | tf_op jit(solution)/shard_map/psum | solution.py:156
  623.1 0.9 copy-start.6
  623.2 0.9 copy-start.9
  918.5 3.7 copy-start.4
  918.5 3.7 copy-start.7
  918.5 3.7 copy-start.10
  921.4 110.6 %reduce-scatter.2.cloned.1.call-start = ((), (), s32[]{:S(2)}) async-start(), calls=%async_computation.2 | async-start | bytes 2359296 | tf_op jit(solution)/shard_map/reduce_scatter | solution.py:162
Sparse Core Ops, SparseCore 0:
  12.8 492.8 all-gather.8
  509.2 291.1 all-gather.6
  921.5 66.5 all-reduce.2
  991.5 40.4 reduce-scatter.1
